TPU v7x, 32 devices: a whole 2x2x4 slice. The times are simulated.
32 devices in a mesh: dp: 4 (over y, x), expert: 8 (over z, core).
Axes of the slice: x: 2, y: 2, z: 4, core: 2. Of those that a mesh axis runs over, the one named last changes fastest.
Arguments:
- output_grad: bfloat16 [6144, 2048], P(('dp', 'expert')), may hold values from -3 to 3
- routes: int32 [6144, 2], P(('dp', 'expert')), may hold values from 0 to 7, all different within a row; in each aligned block of 192 rows (0 to 191, 192 to 383, ...) at most 72 rows name the same one
- combine_weights: bfloat16 [6144, 2], P(('dp', 'expert')), may hold values from 0.049804688 to 0.5
- saved_hidden: bfloat16 [18432, 768], P(('dp', 'expert')), may hold values from -0.796875 to 0.796875
- down_weight: bfloat16 [8, 768, 2048], P('expert', 'dp'), may hold values from -0.21875 to 0.21875
Outputs:
- hidden_grad: bfloat16 [18432, 768], P(('dp', 'expert'))
- weight_grad: float32 [8, 768, 2048], P('expert', 'dp')
- route_grad: float32 [6144, 2], P(('dp', 'expert'))
Inputs may be any that keep to these rules, and one draw needn't show every extreme that they name: Each token names 2 different experts; among the 192 rows of one device no expert is named by more than 72 routes.
All inputs are finite; a program needn't handle non-finite values.
Results may differ from a plain program's by a relative error of at most 0.008.
Values may be sent and summed in bfloat16 or wider, within the bound.
A program may use at most 64 MiB of HBM per device.

v0:
```python
import jax
import jax.numpy as jnp
from jax import lax
from jax.sharding import PartitionSpec as P


def route_slots(routes, experts, capacity):
    flat_ids = routes.reshape(-1)
    place = jnp.arange(flat_ids.shape[0], dtype=jnp.int32)
    same = flat_ids[:, None] == flat_ids[None, :]
    rank = jnp.sum((same & (place[None, :] < place[:, None])).astype(jnp.int32), axis=1)
    return flat_ids * capacity + rank


def per_device(output_grad, routes, combine_weights, saved_hidden, down_weight):
    experts = lax.axis_size("expert")
    slot_count = saved_hidden.shape[0]
    capacity = slot_count // experts
    features = output_grad.shape[1]
    route_total = routes.shape[0] * routes.shape[1]
    target = route_slots(routes, experts, capacity)
    source = (
        jnp.full((slot_count,), route_total, jnp.int32)
        .at[target]
        .set(jnp.arange(route_total, dtype=jnp.int32))
    )
    is_live = source < route_total
    safe_index = jnp.where(is_live, source, 0)
    send_rows = jnp.where(
        is_live[:, None], output_grad[safe_index // routes.shape[1]], jnp.zeros((), jnp.bfloat16)
    )
    send_weights = jnp.where(
        is_live, combine_weights.reshape(-1)[safe_index], jnp.zeros((), jnp.bfloat16)
    )
    recv_rows, recv_weights = (
        lax.all_to_all(
            send_rows.reshape(experts, capacity, features),
            "expert",
            split_axis=0,
            concat_axis=0,
            tiled=True,
        ),
        lax.all_to_all(
            send_weights.reshape(experts, capacity),
            "expert",
            split_axis=0,
            concat_axis=0,
            tiled=True,
        ),
    )
    grad_rows = recv_rows.reshape(slot_count, features)
    slot_weights = recv_weights.reshape(slot_count).astype(jnp.float32)
    weighted = (slot_weights[:, None] * grad_rows.astype(jnp.float32)).astype(jnp.bfloat16)
    weight_shard = down_weight[0]
    contract = (((1,), (1,)), ((), ()))
    full_weight = lax.all_gather(weight_shard, "dp", axis=0, tiled=True)
    unscaled = lax.dot_general(grad_rows, full_weight, contract, preferred_element_type=jnp.float32)
    route_terms = jnp.sum(saved_hidden.astype(jnp.float32) * unscaled, axis=1)
    hidden_grad = (slot_weights[:, None] * unscaled).astype(jnp.bfloat16)
    grad_part = lax.psum_scatter(
        lax.dot_general(
            saved_hidden, weighted, (((0,), (0,)), ((), ())), preferred_element_type=jnp.float32
        ).astype(jnp.bfloat16),
        "dp",
        scatter_dimension=0,
        tiled=True,
    ).astype(jnp.float32)
    returned = lax.all_to_all(
        route_terms.reshape(experts, capacity), "expert", split_axis=0, concat_axis=0, tiled=True
    )
    route_grad = returned.reshape(-1)[target].reshape(routes.shape)
    return (hidden_grad, grad_part[None], route_grad)


def solution(mesh):
    return jax.shard_map(
        per_device,
        mesh=mesh,
        in_specs=(
            P(("dp", "expert"), None),
            P(("dp", "expert"), None),
            P(("dp", "expert"), None),
            P(("dp", "expert"), None),
            P("expert", "dp", None),
        ),
        out_specs=(P(("dp", "expert"), None), P("expert", "dp", None), P(("dp", "expert"), None)),
        check_vma=False,
    )
```

profile of v0, /device:TPU:0, one launch (start us, length us, event | category | flops | bytes accessed | tf_op | source)
XLA Modules:
  0.0 155.5 jit_solution(9721528789717610883)
XLA Ops:
  7.2 0.0 copy-start
  7.2 0.9 copy.21
  8.1 0.7 broadcast_multiply_fusion
  8.7 0.1 eq.15
  8.9 0.2 convert_reduce_fusion
  9.1 0.1 copy.20
  9.2 0.1 mul.37
  9.4 2.9 %scatter_custom_fusion = s32[576]{0:T(1024)S(1)} fusion(s32[384]{0:T(512)S(1)} %fusion.9, s32[384]{0:T(512)S(1)} %iota.10, s32[]{:T(128)} %constant.9.clone.1), kind=kCustom, calls=%fused_computation.32 | custom fusion | bytes 2308 | tf_op jit(solution)/shard_map/scatter | solution.py:25
  12.4 0.8 copy.22
  13.2 0.2 reshape.75
  13.4 3.9 %gather_fusion = bf16[576]{0:T(1024)(128)(2,1)S(1)} fusion(bf16[384]{0:T(512)(128)(2,1)S(1)} %reshape.75, s32[1024]{0:T(1024)S(1)} %pad_clamp_fusion.2), kind=kCustom, calls=%fused_computation | custom fusion | bytes 4608 | tf_op jit(solution)/shard_map/gather | solution.py:33
  17.3 0.7 all_to_all.20
  18.0 6.3 %all-to-all-start = ((bf16[8,1,72]{2,1,0:T(2,128)(2,1)}), bf16[8,1,72]{2,1,0:T(2,128)(2,1)S(1)}, u32[]{:S(2)}, u32[]{:S(2)}) async-start(bf16[8,1,72]{2,1,0:T(2,128)(2,1)} %all_to_all.20), calls=%async_computation | async-start | bytes 8192 | tf_op jit(solution)/shard_map/all_to_all | solution.py:43
  24.3 0.0 all-gather.3.cloned.1.call-start
  24.4 0.7 all-gather.3.cloned.1.call-update
  25.1 0.1 broadcast_in_dim.44
  25.2 0.0 copy-done
  25.2 3.4 %gather_fusion.1 = bf16[576,2048]{1,0:T(8,128)(2,1)S(1)} fusion(bf16[192,2048]{1,0:T(8,128)(2,1)S(1)} %copy-done, s32[1024]{0:T(1024)S(1)} %pad_clamp_fusion.1), kind=kCustom, calls=%fused_computation.1 | custom fusion | bytes 4720896 | tf_op jit(solution)/shard_map/gather | solution.py:30
  28.6 1.7 %broadcast_select_fusion = bf16[8,72,2048]{2,1,0:T(8,128)(2,1)} fusion(bf16[8,72,2048]{2,1,0:T(8,128)(2,1)S(1)} %bitcast.15, pred[8,72]{1,0:T(8,128)(4,1)S(1)} %broadcast_in_dim.44), kind=kLoop, calls=%fused_computation.10 | loop fusion | flops 1179648 | bytes 4719168 | tf_op jit(solution)/shard_map/jit(_where)/select_n | solution.py:29
  30.3 0.0 all-to-all-done
  30.3 5.1 %all-to-all-start.1 = ((bf16[8,72,2048]{2,1,0:T(8,128)(2,1)}), bf16[8,72,2048]{2,1,0:T(8,128)(2,1)S(1)}, u32[]{:S(2)}, u32[]{:S(2)}) async-start(bf16[8,72,2048]{2,1,0:T(8,128)(2,1)} %broadcast_select_fusion), calls=%async_computation.1 | async-start | bytes 4718592 | tf_op jit(solution)/shard_map/all_to_all | solution.py:36
  35.4 0.0 reduce-scatter.4.cloned.1.call-start
  35.5 0.1 reshape.79
  35.5 54.5 %all-to-all-done.1 = bf16[8,72,2048]{2,1,0:T(8,128)(2,1)S(1)} async-done(((bf16[8,72,2048]{2,1,0:T(8,128)(2,1)}), bf16[8,72,2048]{2,1,0:T(8,128)(2,1)S(1)}, u32[]{:S(2)}, u32[]{:S(2)}) %all-to-all-start.1) | async-done | bytes 2359328 | tf_op jit(solution)/shard_map/all_to_all | solution.py:36
  90.1 5.5 %fusion.2 = bf16[768,2048]{0,1:T(8,128)(2,1)} fusion(bf16[576,768]{1,0:T(8,128)(2,1)} %param.8, bf16[576,2048]{1,0:T(8,128)(2,1)S(1)} %bitcast.16, f32[576]{0:T(1024)S(1)} %reshape.79), kind=kOutput, calls=%fused_computation.8 | convolution fusion | flops 1817051136 | bytes 6392064 | tf_op jit(solution)/shard_map/dot_general | solution.py:61
  95.6 4.7 %copy.26 = bf16[768,2048]{1,0:T(8,128)(2,1)} copy(bf16[768,2048]{0,1:T(8,128)(2,1)} %fusion.2) | data formatting | bytes 6291456
  100.3 0.0 reduce-scatter.4.cloned.1.call-update
  100.3 0.0 all-gather.3.cloned.1.call-done
  100.3 5.1 %multiply_reduce_fusion = (f32[576]{0:T(1024)S(1)}, bf16[576,768]{1,0:T(8,128)(2,1)}) fusion(bf16[576,768]{1,0:T(8,128)(2,1)} %param.8, f32[576]{0:T(1024)S(1)} %reshape.79, bf16[576,2048]{1,0:T(8,128)(2,1)S(1)} %bitcast.17, bf16[1,768,2048]{2,1,0:T(8,128)(2,1)} %all-gather.3.cloned.1.call-done), kind=kOutput, calls=%fused_computation.11 | convolution fusion | flops 1814150656 | bytes 7279104 | tf_op jit(solution)/shard_map/dot_general | solution.py:57
  105.4 0.7 all_to_all.18
  106.1 3.3 %all-to-all-start.2 = ((f32[8,1,72]{2,1,0:T(1,128)}), f32[8,1,72]{2,1,0:T(1,128)S(1)}, u32[]{:S(2)}, u32[]{:S(2)}) async-start(f32[8,1,72]{2,1,0:T(1,128)} %all_to_all.18), calls=%async_computation.2 | async-start | bytes 8192 | tf_op jit(solution)/shard_map/all_to_all | solution.py:68
  109.4 5.4 %all-to-all-done.2 = f32[8,1,72]{2,1,0:T(1,128)S(1)} async-done(((f32[8,1,72]{2,1,0:T(1,128)}), f32[8,1,72]{2,1,0:T(1,128)S(1)}, u32[]{:S(2)}, u32[]{:S(2)}) %all-to-all-start.2) | async-done | bytes 2336 | tf_op jit(solution)/shard_map/all_to_all | solution.py:68
  114.8 0.5 broadcast.69
  115.3 0.7 reduce.9
  116.0 0.1 reshape.77
  116.1 1.9 %gather_fusion.2 = f32[384]{0:T(512)S(1)} fusion(f32[576]{0:T(1024)S(1)} %reshape.77, s32[1024]{0:T(1024)S(1)} %pad_clamp_fusion), kind=kCustom, calls=%fused_computation.2 | custom fusion | bytes 4608 | tf_op jit(solution)/shard_map/gather | solution.py:71
  118.0 0.1 reshape.78
  118.1 0.7 copy.25
  118.8 24.6 %reduce-scatter.4.cloned.1.call-done = bf16[192,2048]{1,0:T(8,128)(2,1)} async-done(((bf16[768,2048]{1,0:T(8,128)(2,1)}), bf16[192,2048]{1,0:T(8,128)(2,1)}) %reduce-scatter.4.cloned.1.call-update) | async-done | bytes 786448
  143.3 2.2 %copy.27 = bf16[192,2048]{0,1:T(8,128)(2,1)} copy(bf16[192,2048]{1,0:T(8,128)(2,1)} %reduce-scatter.4.cloned.1.call-done) | data formatting | bytes 1572864
  145.6 1.4 bitcast_convert_fusion
  146.9 1.7 %copy.24 = f32[1,192,2048]{2,1,0:T(8,128)} copy(f32[1,192,2048]{1,2,0:T(8,128)S(1)} %bitcast_convert_fusion) | data formatting | bytes 3145728
  (9 shorter events, 0.1 us)
Async XLA Ops:
  7.2 18.0 %copy-start = (bf16[192,2048]{1,0:T(8,128)(2,1)S(1)}, bf16[192,2048]{1,0:T(8,128)(2,1)}, u32[]{:S(2)}) copy-start(bf16[192,2048]{1,0:T(8,128)(2,1)} %param.5) | copy-start | bytes 2359300
  18.0 12.3 %all-to-all-start = ((bf16[8,1,72]{2,1,0:T(2,128)(2,1)}), bf16[8,1,72]{2,1,0:T(2,128)(2,1)S(1)}, u32[]{:S(2)}, u32[]{:S(2)}) async-start(bf16[8,1,72]{2,1,0:T(2,128)(2,1)} %all_to_all.20), calls=%async_computation | async-start | bytes 8192 | tf_op jit(solution)/shard_map/all_to_all | solution.py:43
  24.3 76.0 %all-gather.3.cloned.1.call-start = ((), (), s32[]{:S(2)}) async-start(), calls=%async_computation.4 | async-start | bytes 3932160 | tf_op jit(solution)/shard_map/all_gather | solution.py:56
  30.3 59.8 %all-to-all-start.1 = ((bf16[8,72,2048]{2,1,0:T(8,128)(2,1)}), bf16[8,72,2048]{2,1,0:T(8,128)(2,1)S(1)}, u32[]{:S(2)}, u32[]{:S(2)}) async-start(bf16[8,72,2048]{2,1,0:T(8,128)(2,1)} %broadcast_select_fusion), calls=%async_computation.1 | async-start | bytes 4718592 | tf_op jit(solution)/shard_map/all_to_all | solution.py:36
  35.4 108.0 %reduce-scatter.4.cloned.1.call-start = ((), (), s32[]{:S(2)}) async-start(), calls=%async_computation.5 | async-start | bytes 3932160
  106.1 8.7 %all-to-all-start.2 = ((f32[8,1,72]{2,1,0:T(1,128)}), f32[8,1,72]{2,1,0:T(1,128)S(1)}, u32[]{:S(2)}, u32[]{:S(2)}) async-start(f32[8,1,72]{2,1,0:T(1,128)} %all_to_all.18), calls=%async_computation.2 | async-start | bytes 8192 | tf_op jit(solution)/shard_map/all_to_all | solution.py:68
Sparse Core Ops, SparseCore 0:
  27.0 45.4 all-gather.2
  100.4 42.8 reduce-scatter.3
where the time goes:
time: 156 us; the launch traced here: 155 us
  waiting for transfers between devices  85.2 us (55%)
  local copies, waits for them, and re-layouts  25.9 us (17%)
  starting transfers between devices  14.8 us (9%)
  between operations  14.2 us (9%)
  matrix products  10.6 us (7%)
  other arithmetic  4.73 us (3%)
    all_to_all x1, waiting for transfers between devices, per_device(): lax.all_to_all(send_rows.reshape(experts, capacity, features), 'expert',...  54.5 us
    unnamed x3, waiting for transfers between devices  25.3 us
    unnamed x8, local copies, waits for them, and re-layouts  11 us
    all_to_all x1, starting transfers between devices, per_device(): lax.all_to_all(send_weights.reshape(experts, capacity), 'expert', split_a...  6.33 us
    dot_general x1, matrix products, per_device(): lax.dot_general(saved_hidden, weighted, (((0,), (0,)), ((), ())), preferr...  5.51 us
    all_to_all x1, waiting for transfers between devices, per_device(): lax.all_to_all(route_terms.reshape(experts, capacity), 'expert', split_ax...  5.4 us
    all_to_all x1, starting transfers between devices, per_device(): lax.all_to_all(send_rows.reshape(experts, capacity, features), 'expert',...  5.09 us
    dot_general x1, matrix products, per_device(): lax.dot_general(grad_rows, full_weight, contract, preferred_element_type=...  5.08 us
  transfers between devices with their start and end apart: 5, of which 3 were waited for; matrix products, arithmetic and copies ran while one was open for 16% of the time, Pallas kernels for 0%

commit v1 on v0

--- a/solution.py
+++ b/solution.py
@@ -2,6 +2,30 @@
 import jax.numpy as jnp
 from jax import lax
 from jax.sharding import PartitionSpec as P
+
+
+def in_blocks(array, dim, size):
+    shape = array.shape
+    blocks = array.reshape(*shape[:dim], size, shape[dim] // size, *shape[dim + 1 :])
+    return jnp.moveaxis(blocks, dim, 0)
+
+
+def laid_out(pieces, dim):
+    pieces = jnp.moveaxis(pieces, 0, dim)
+    shape = pieces.shape
+    return pieces.reshape(*shape[:dim], shape[dim] * shape[dim + 1], *shape[dim + 2 :])
+
+
+def rotated_exchange(shard, axis, split_dim, concat_dim):
+    size, place = (lax.axis_size(axis), lax.axis_index(axis))
+    blocks = in_blocks(shard, split_dim, size)
+    out = blocks
+    for turn in range(1, size):
+        target, source = ((place + turn) % size, (place - turn) % size)
+        sent = lax.dynamic_index_in_dim(blocks, target, 0)
+        theirs = lax.ppermute(sent, axis, [(i, (i + turn) % size) for i in range(size)])
+        out = lax.dynamic_update_slice_in_dim(out, theirs, source, axis=0)
+    return laid_out(out, concat_dim)
 
 
 def route_slots(routes, experts, capacity):
@@ -33,13 +57,7 @@
         is_live, combine_weights.reshape(-1)[safe_index], jnp.zeros((), jnp.bfloat16)
     )
     recv_rows, recv_weights = (
-        lax.all_to_all(
-            send_rows.reshape(experts, capacity, features),
-            "expert",
-            split_axis=0,
-            concat_axis=0,
-            tiled=True,
-        ),
+        rotated_exchange(send_rows.reshape(experts, capacity, features), "expert", 0, 0),
         lax.all_to_all(
             send_weights.reshape(experts, capacity),
             "expert",

time: 156 us -> 147 us (0.942)
  waiting for transfers between devices: 85.2 us -> 59.6 us
  starting transfers between devices: 14.8 us -> 29.2 us
  local copies, waits for them, and re-layouts: 25.9 us -> 30.8 us
    all_to_all x1 -> x0, waiting for transfers between devices: 54.5 us -> none  [per_device(): lax.all_to_all(send_rows.reshape(experts, capacity, features), 'expert',...]
    ppermute x0 -> x7, waiting for transfers between devices: none -> 23.7 us  [rotated_exchange(): lax.ppermute(sent, axis, [(i, (i + turn) % size) for i in range(size)])]
    all_to_all x1, starting transfers between devices: 3.31 us -> 17.7 us  [per_device(): lax.all_to_all(route_terms.reshape(experts, capacity), 'expert', split_ax...]
    ppermute x0 -> x7, starting transfers between devices: none -> 6.59 us  [rotated_exchange(): lax.ppermute(sent, axis, [(i, (i + turn) % size) for i in range(size)])]
    all_to_all x1 -> x0, starting transfers between devices: 5.09 us -> none  [per_device(): lax.all_to_all(send_rows.reshape(experts, capacity, features), 'expert',...]
    all_to_all x1, waiting for transfers between devices: 0.01 us -> 3.89 us  [per_device(): lax.all_to_all(send_weights.reshape(experts, capacity), 'expert', split_a...]
    dynamic_slice x0 -> x2, local copies, waits for them, and re-layouts: none -> 2.11 us  [rotated_exchange(): sent = lax.dynamic_index_in_dim(blocks, target, 0)]
    dynamic_update_slice x0 -> x6, local copies, waits for them, and re-layouts: none -> 2.06 us  [rotated_exchange(): out = lax.dynamic_update_slice_in_dim(out, theirs, source, axis=0)]
  transfers between devices with their start and end apart: 5 -> 11, of which waited for: 3 -> 7; matrix products, arithmetic and copies ran while one was open for 16% -> 24% of each run, Pallas kernels for 0% -> 0%
where the time goes in v1:
time: 147 us
  waiting for transfers between devices  59.6 us (41%)
  local copies, waits for them, and re-layouts  30.8 us (21%)
  starting transfers between devices  29.2 us (20%)
  between operations  14.5 us (10%)
  matrix products  9.48 us (6%)
  other arithmetic  3.28 us (2%)
    unnamed x3, waiting for transfers between devices  26.5 us
    ppermute x7, waiting for transfers between devices, rotated_exchange(): lax.ppermute(sent, axis, [(i, (i + turn) % size) for i in range(size)])  23.7 us
    all_to_all x1, starting transfers between devices, per_device(): lax.all_to_all(route_terms.reshape(experts, capacity), 'expert', split_ax...  17.7 us
    unnamed x16, local copies, waits for them, and re-layouts  11.7 us
    ppermute x7, starting transfers between devices, rotated_exchange(): lax.ppermute(sent, axis, [(i, (i + turn) % size) for i in range(size)])  6.59 us
    all_to_all x1, waiting for transfers between devices, per_device(): lax.all_to_all(route_terms.reshape(experts, capacity), 'expert', split_ax...  5.47 us
    dot_general x1, matrix products, per_device(): lax.dot_general(grad_rows, full_weight, contract, preferred_element_type=...  5.08 us
    all_to_all x1, starting transfers between devices, per_device(): lax.all_to_all(send_weights.reshape(experts, capacity), 'expert', split_a...  4.83 us
  transfers between devices with their start and end apart: 11, of which 7 were waited for; matrix products, arithmetic and copies ran while one was open for 24% of the time, Pallas kernels for 0%

profile of v1, /device:TPU:0, one launch (start us, length us, event | category | flops | bytes accessed | tf_op | source)
XLA Modules:
  0.0 146.8 jit_solution(18272878021030348113)
XLA Ops:
  7.2 0.7 all-gather.3.cloned.1.call-update
  7.9 0.8 copy.21
  8.7 0.7 broadcast_multiply_fusion
  9.4 0.1 copy.20
  9.5 0.1 mul.37
  9.7 0.1 eq.30
  9.8 0.2 convert_reduce_fusion
  10.1 2.9 %scatter_custom_fusion = s32[576]{0:T(1024)S(1)} fusion(s32[384]{0:T(512)S(1)} %fusion.9, s32[384]{0:T(512)S(1)} %iota.10, s32[]{:T(128)} %constant.114.clone.1), kind=kCustom, calls=%fused_computation.46 | custom fusion | bytes 2308 | tf_op jit(solution)/shard_map/scatter | solution.py:49
  13.1 0.1 broadcast_in_dim.44
  13.2 3.4 %gather_fusion.1 = bf16[576,2048]{1,0:T(8,128)(2,1)S(1)} fusion(bf16[192,2048]{1,0:T(8,128)(2,1)S(1)} %copy-done, s32[1024]{0:T(1024)S(1)} %pad_clamp_fusion.1), kind=kCustom, calls=%fused_computation.1 | custom fusion | bytes 4720896 | tf_op jit(solution)/shard_map/gather | solution.py:54
  16.6 0.2 broadcast_select_fusion
  16.9 1.4 copy-done.1
  18.3 0.5 collective-permute-start
  18.8 0.1 copy.22
  19.0 0.2 reshape.82
  19.2 3.9 %gather_fusion = bf16[576]{0:T(1024)(128)(2,1)S(1)} fusion(bf16[384]{0:T(512)(128)(2,1)S(1)} %reshape.82, s32[1024]{0:T(1024)S(1)} %pad_clamp_fusion.2), kind=kCustom, calls=%fused_computation | custom fusion | bytes 4608 | tf_op jit(solution)/shard_map/gather | solution.py:57
  23.2 4.2 %collective-permute-done = bf16[1,1,72,2048]{3,2,0,1:T(8,128)(2,1)} collective-permute-done((bf16[1,1,72,2048]{3,2,0,1:T(8,128)(2,1)S(1)}, bf16[1,1,72,2048]{3,2,0,1:T(8,128)(2,1)}, u32[]{:S(2)}, u32[]{:S(2)}) %collective-permute-start) | collective-permute-done | bytes 294944 | tf_op jit(solution)/shard_map/ppermute | solution.py:26
  27.4 2.1 %constant_dynamic-slice_fusion = (bf16[1,1,72,2048]{3,2,0,1:T(8,128)(2,1)S(1)}, bf16[1,1,72,2048]{3,2,0,1:T(8,128)(2,1)}, bf16[1,1,72,2048]{3,2,0,1:T(8,128)(2,1...) fusion(bf16[8,1,72,2048]{3,2,0,1:T(8,128)(2,1)S(1)} %copy-done., ...), kind=kLoop, calls=%fused_computation.32 | loop fusion | bytes 4128796 | tf_op jit(solution)/shard_map/jit(dynamic_index_in_dim)/dynamic_slice | solution.py:25
  29.5 0.3 collective-permute-start.1
  29.8 0.7 all_to_all.16
  30.4 4.8 %all-to-all-start = ((bf16[8,1,72]{2,1,0:T(2,128)(2,1)}), bf16[8,1,72]{2,1,0:T(2,128)(2,1)S(1)}, u32[]{:S(2)}, u32[]{:S(2)}) async-start(bf16[8,1,72]{2,1,0:T(2,128)(2,1)} %all_to_all.16), calls=%async_computation | async-start | bytes 8192 | tf_op jit(solution)/shard_map/all_to_all | solution.py:61
  35.4 1.6 %collective-permute-start.2 = (bf16[1,1,72,2048]{3,2,0,1:T(8,128)(2,1)}, bf16[1,1,72,2048]{3,2,0,1:T(8,128)(2,1)}, u32[]{:S(2)}, u32[]{:S(2)}) collective-permute-start(bf16[1,1,72,2048]{3,2,0,1:T(8,128)(2,1)} %get-tuple-element.21), channel_id=1, source_target_pairs={{0,3},{1,4},{2,5},{3,6},{4,7},{5,0},{6,1},{7,2},{8,11},{9,12},{10,... | collective-permute-start | bytes 884744 | tf_op jit(solution)/shard_map/ppermute | solution.py:26
  37.0 3.9 %all-to-all-done = bf16[8,1,72]{2,1,0:T(2,128)(2,1)S(1)} async-done(((bf16[8,1,72]{2,1,0:T(2,128)(2,1)}), bf16[8,1,72]{2,1,0:T(2,128)(2,1)S(1)}, u32[]{:S(2)}, u32[]{:S(2)}) %all-to-all-start) | async-done | bytes 1184 | tf_op jit(solution)/shard_map/all_to_all | solution.py:61
  41.0 0.1 reshape.85
  41.0 0.5 collective-permute-start.3
  41.6 1.6 %collective-permute-start.4 = (bf16[1,1,72,2048]{3,2,0,1:T(8,128)(2,1)}, bf16[1,1,72,2048]{3,2,0,1:T(8,128)(2,1)S(1)}, u32[]{:S(2)}, u32[]{:S(2)}) collective-permute-start(bf16[1,1,72,2048]{3,2,0,1:T(8,128)(2,1)} %get-tuple-element.19), channel_id=1, source_target_pairs={{0,5},{1,6},{2,7},{3,0},{4,1},{5,2},{6,3},{7,4},{8,13},{9,14},{10,... | collective-permute-start | bytes 884744 | tf_op jit(solution)/shard_map/ppermute | solution.py:26
  43.2 0.9 collective-permute-start.5
  44.1 1.2 collective-permute-start.6
  45.2 1.0 constant_dynamic-update-slice_fusion.5
  46.2 14.4 %collective-permute-done.2 = bf16[1,1,72,2048]{3,2,0,1:T(8,128)(2,1)} collective-permute-done((bf16[1,1,72,2048]{3,2,0,1:T(8,128)(2,1)}, bf16[1,1,72,2048]{3,2,0,1:T(8,128)(2,1)}, u32[]{:S(2)}, u32[]{:S(2)}) %collective-permute-start.2) | collective-permute-done | bytes 294944 | tf_op jit(solution)/shard_map/ppermute | solution.py:26
  60.6 1.0 constant_dynamic-update-slice_fusion.4
  61.6 1.6 %collective-permute-done.3 = bf16[1,1,72,2048]{3,2,0,1:T(8,128)(2,1)S(1)} collective-permute-done((bf16[1,1,72,2048]{3,2,0,1:T(8,128)(2,1)}, bf16[1,1,72,2048]{3,2,0,1:T(8,128)(2,1)S(1)}, u32[]{:S(2)}, u32[]{:S(2)}) %collective-permute-start.3) | collective-permute-done | bytes 294944 | tf_op jit(solution)/shard_map/ppermute | solution.py:26
  63.4 3.4 %collective-permute-done.6 = bf16[1,1,72,2048]{3,2,0,1:T(8,128)(2,1)S(1)} collective-permute-done((bf16[1,1,72,2048]{3,2,0,1:T(8,128)(2,1)S(1)}, bf16[1,1,72,2048]{3,2,0,1:T(8,128)(2,1)S(1)}, u32[]{:S(2)}, u32[]{:S(2)}) %collective-permute-start.6) | collective-permute-done | bytes 294944 | tf_op jit(solution)/shard_map/ppermute | solution.py:26
  66.8 4.4 %fusion.2 = bf16[768,2048]{0,1:T(8,128)(2,1)} fusion(bf16[576,768]{1,0:T(8,128)(2,1)S(1)} %copy-done.4, bf16[576,2048]{1,0:T(8,128)(2,1)S(1)} %bitcast.16, f32[576]{0:T(1024)S(1)} %reshape.85), kind=kOutput, calls=%fused_computation.8 | convolution fusion | flops 1817051136 | bytes 6392064 | tf_op jit(solution)/shard_map/dot_general | solution.py:79
  71.2 4.7 %copy.26 = bf16[768,2048]{1,0:T(8,128)(2,1)} copy(bf16[768,2048]{0,1:T(8,128)(2,1)} %fusion.2) | data formatting | bytes 6291456
  76.0 5.1 %multiply_reduce_fusion = (f32[576]{0:T(1024)S(1)}, bf16[576,768]{1,0:T(8,128)(2,1)}) fusion(bf16[576,768]{1,0:T(8,128)(2,1)} %param.8, f32[576]{0:T(1024)S(1)} %reshape.85, bf16[576,2048]{1,0:T(8,128)(2,1)S(1)} %bitcast.17, bf16[1,768,2048]{2,1,0:T(8,128)(2,1)} %all-gather.3.cloned.1.call-done), kind=kOutput, calls=%fused_computation.11 | convolution fusion | flops 1814150656 | bytes 7279104 | tf_op jit(solution)/shard_map/dot_general | solution.py:75
  81.1 0.7 all_to_all.14
  81.7 17.7 %all-to-all-start.1 = ((f32[8,1,72]{2,1,0:T(1,128)}), f32[8,1,72]{2,1,0:T(1,128)S(1)}, u32[]{:S(2)}, u32[]{:S(2)}) async-start(f32[8,1,72]{2,1,0:T(1,128)} %all_to_all.14), calls=%async_computation.1 | async-start | bytes 8192 | tf_op jit(solution)/shard_map/all_to_all | solution.py:86
  99.5 5.5 %all-to-all-done.1 = f32[8,1,72]{2,1,0:T(1,128)S(1)} async-done(((f32[8,1,72]{2,1,0:T(1,128)}), f32[8,1,72]{2,1,0:T(1,128)S(1)}, u32[]{:S(2)}, u32[]{:S(2)}) %all-to-all-start.1) | async-done | bytes 2336 | tf_op jit(solution)/shard_map/all_to_all | solution.py:86
  104.9 0.5 broadcast.100
  105.5 0.7 reduce.9
  106.2 1.9 %gather_fusion.2 = f32[384]{0:T(512)S(1)} fusion(f32[576]{0:T(1024)S(1)} %reshape.83, s32[1024]{0:T(1024)S(1)} %pad_clamp_fusion), kind=kCustom, calls=%fused_computation.2 | custom fusion | bytes 4608 | tf_op jit(solution)/shard_map/gather | solution.py:89
  108.1 0.1 reshape.84
  108.2 0.7 copy.25
  108.9 25.8 %reduce-scatter.4.cloned.1.call-done = bf16[192,2048]{1,0:T(8,128)(2,1)} async-done(((bf16[768,2048]{1,0:T(8,128)(2,1)}), bf16[192,2048]{1,0:T(8,128)(2,1)}) %reduce-scatter.4.cloned.1.call-update) | async-done | bytes 786448
  134.7 2.2 %copy.27 = bf16[192,2048]{0,1:T(8,128)(2,1)} copy(bf16[192,2048]{1,0:T(8,128)(2,1)} %reduce-scatter.4.cloned.1.call-done) | data formatting | bytes 1572864
  136.9 1.4 bitcast_convert_fusion
  138.3 1.7 %copy.24 = f32[1,192,2048]{2,1,0:T(8,128)} copy(f32[1,192,2048]{1,2,0:T(8,128)S(1)} %bitcast_convert_fusion) | data formatting | bytes 3145728
  (31 shorter events, 0.4 us)
Async XLA Ops:
  7.2 6.0 %copy-start = (bf16[192,2048]{1,0:T(8,128)(2,1)S(1)}, bf16[192,2048]{1,0:T(8,128)(2,1)}, u32[]{:S(2)}) copy-start(bf16[192,2048]{1,0:T(8,128)(2,1)} %param.5) | copy-start | bytes 2359300
  7.2 68.8 %all-gather.3.cloned.1.call-start = ((), (), s32[]{:S(2)}) async-start(), calls=%async_computation.3 | async-start | bytes 3932160 | tf_op jit(solution)/shard_map/all_gather | solution.py:74
  16.6 2.2 %copy-start.3 = (bf16[192,2]{0,1:T(2,128)(2,1)S(1)}, bf16[192,2]{0,1:T(2,128)(2,1)}, u32[]{:S(2)}) copy-start(bf16[192,2]{0,1:T(2,128)(2,1)} %param.7) | copy-start | bytes 2308
  16.9 1.5 copy-start.1
  18.3 9.1 %copy-start.2 = (bf16[8,1,72,2048]{3,2,0,1:T(8,128)(2,1)S(1)}, bf16[8,1,72,2048]{3,2,0,1:T(8,128)(2,1)}, u32[]{:S(2)}) copy-start(bf16[8,1,72,2048]{3,2,0,1:T(8,128)(2,1)} %copy-done.1) | copy-start | bytes 7077892
  18.3 9.1 %collective-permute-start = (bf16[1,1,72,2048]{3,2,0,1:T(8,128)(2,1)S(1)}, bf16[1,1,72,2048]{3,2,0,1:T(8,128)(2,1)}, u32[]{:S(2)}, u32[]{:S(2)}) collective-permute-start(bf16[1,1,72,2048]{3,2,0,1:T(8,128)(2,1)S(1)} %constant_dynamic-slice_fusion.6), channel_id=1, source_target_pairs={{0,1},{1,2},{2,3},{3,4},{4,5},{5,6},{6,7},{7,0},{8,9},{9,10},{10,1... | collective-permute-start | bytes 884744 | tf_op jit(solution)/shard_map/ppermute | solution.py:26
  29.5 14.6 %collective-permute-start.1 = (bf16[1,1,72,2048]{3,2,0,1:T(8,128)(2,1)}, bf16[1,1,72,2048]{3,2,0,1:T(8,128)(2,1)}, u32[]{:S(2)}, u32[]{:S(2)}) collective-permute-start(bf16[1,1,72,2048]{3,2,0,1:T(8,128)(2,1)} %get-tuple-element.22), channel_id=1, source_target_pairs={{0,2},{1,3},{2,4},{3,5},{4,6},{5,7},{6,0},{7,1},{8,10},{9,11},{10,... | collective-permute-start | bytes 884744 | tf_op jit(solution)/shard_map/ppermute | solution.py:26
  30.4 10.5 %all-to-all-start = ((bf16[8,1,72]{2,1,0:T(2,128)(2,1)}), bf16[8,1,72]{2,1,0:T(2,128)(2,1)S(1)}, u32[]{:S(2)}, u32[]{:S(2)}) async-start(bf16[8,1,72]{2,1,0:T(2,128)(2,1)} %all_to_all.16), calls=%async_computation | async-start | bytes 8192 | tf_op jit(solution)/shard_map/all_to_all | solution.py:61
  35.3 99.4 %reduce-scatter.4.cloned.1.call-start = ((), (), s32[]{:S(2)}) async-start(), calls=%async_computation.4 | async-start | bytes 3932160
  35.4 25.2 %collective-permute-start.2 = (bf16[1,1,72,2048]{3,2,0,1:T(8,128)(2,1)}, bf16[1,1,72,2048]{3,2,0,1:T(8,128)(2,1)}, u32[]{:S(2)}, u32[]{:S(2)}) collective-permute-start(bf16[1,1,72,2048]{3,2,0,1:T(8,128)(2,1)} %get-tuple-element.21), channel_id=1, source_target_pairs={{0,3},{1,4},{2,5},{3,6},{4,7},{5,0},{6,1},{7,2},{8,11},{9,12},{10,... | collective-permute-start | bytes 884744 | tf_op jit(solution)/shard_map/ppermute | solution.py:26
  41.0 25.8 %copy-start.4 = (bf16[576,768]{1,0:T(8,128)(2,1)S(1)}, bf16[576,768]{1,0:T(8,128)(2,1)}, u32[]{:S(2)}) copy-start(bf16[576,768]{1,0:T(8,128)(2,1)} %param.8) | copy-start | bytes 2654212
  41.0 22.2 %collective-permute-start.3 = (bf16[1,1,72,2048]{3,2,0,1:T(8,128)(2,1)}, bf16[1,1,72,2048]{3,2,0,1:T(8,128)(2,1)S(1)}, u32[]{:S(2)}, u32[]{:S(2)}) collective-permute-start(bf16[1,1,72,2048]{3,2,0,1:T(8,128)(2,1)} %get-tuple-element.20), channel_id=1, source_target_pairs={{0,4},{1,5},{2,6},{3,7},{4,0},{5,1},{6,2},{7,3},{8,12},{9,13},{10,... | collective-permute-start | bytes 884744 | tf_op jit(solution)/shard_map/ppermute | solution.py:26
  41.6 21.7 %collective-permute-start.4 = (bf16[1,1,72,2048]{3,2,0,1:T(8,128)(2,1)}, bf16[1,1,72,2048]{3,2,0,1:T(8,128)(2,1)S(1)}, u32[]{:S(2)}, u32[]{:S(2)}) collective-permute-start(bf16[1,1,72,2048]{3,2,0,1:T(8,128)(2,1)} %get-tuple-element.19), channel_id=1, source_target_pairs={{0,5},{1,6},{2,7},{3,0},{4,1},{5,2},{6,3},{7,4},{8,13},{9,14},{10,... | collective-permute-start | bytes 884744 | tf_op jit(solution)/shard_map/ppermute | solution.py:26
  43.2 20.2 %collective-permute-start.5 = (bf16[1,1,72,2048]{3,2,0,1:T(8,128)(2,1)}, bf16[1,1,72,2048]{3,2,0,1:T(8,128)(2,1)S(1)}, u32[]{:S(2)}, u32[]{:S(2)}) collective-permute-start(bf16[1,1,72,2048]{3,2,0,1:T(8,128)(2,1)} %get-tuple-element.18), channel_id=1, source_target_pairs={{0,6},{1,7},{2,0},{3,1},{4,2},{5,3},{6,4},{7,5},{8,14},{9,15},{10,... | collective-permute-start | bytes 884744 | tf_op jit(solution)/shard_map/ppermute | solution.py:26
  44.1 22.7 %collective-permute-start.6 = (bf16[1,1,72,2048]{3,2,0,1:T(8,128)(2,1)S(1)}, bf16[1,1,72,2048]{3,2,0,1:T(8,128)(2,1)S(1)}, u32[]{:S(2)}, u32[]{:S(2)}) collective-permute-start(bf16[1,1,72,2048]{3,2,0,1:T(8,128)(2,1)S(1)} %get-tuple-element.17), channel_id=1, source_target_pairs={{0,7},{1,0},{2,1},{3,2},{4,3},{5,4},{6,5},{7,6},{8,15},{9,8},{10,9... | collective-permute-start | bytes 884744 | tf_op jit(solution)/shard_map/ppermute | solution.py:26
  81.7 23.2 %all-to-all-start.1 = ((f32[8,1,72]{2,1,0:T(1,128)}), f32[8,1,72]{2,1,0:T(1,128)S(1)}, u32[]{:S(2)}, u32[]{:S(2)}) async-start(f32[8,1,72]{2,1,0:T(1,128)} %all_to_all.14), calls=%async_computation.1 | async-start | bytes 8192 | tf_op jit(solution)/shard_map/all_to_all | solution.py:86
Sparse Core Ops, SparseCore 0:
  9.9 46.6 all-gather.2
  76.1 58.5 reduce-scatter.3
